TPU v7x, 256 devices: a whole 4x4x8 slice. The times are simulated.
256 devices in a mesh: dp: 4 (over y_lo, core), pipe: 8 (over z), tensor: 8 (over x, y_hi).
Axes of the slice: x: 4, y: 4 (y_hi: 2, y_lo: 2; y = y_hi * 2 + y_lo), z: 8, core: 2. Of those that a mesh axis runs over, the one named last changes fastest.
Arguments:
- checkpoint: bfloat16 [8, 4, 192, 7168], P('pipe', 'dp', None, 'tensor'), may hold values from -6 to 6
- projection: bfloat16 [8, 7168, 3, 7168], P('pipe', 'dp', None, 'tensor'), may hold values from -0.0625 to 0.0625
- ctx_grad: bfloat16 [8, 4, 192, 7168], P('pipe', 'dp', None, 'tensor'), may hold values from -6 to 6
- slopes: float32 [56], P('tensor'), may hold values from 0.003 to 0.1
Outputs:
- input_grad: bfloat16 [8, 4, 192, 7168], P('pipe', 'dp', None, 'tensor')
All inputs are finite; a program needn't handle non-finite values.
Results may differ from a plain program's by a relative error of at most 0.019.
Values may be sent and summed in bfloat16 or wider, within the bound.
No kernel may reach another device: no remote copies, remote signals or barrier semaphores. Data moves between devices by JAX's collectives and lax.ppermute only.
A program may use at most 128 MiB of HBM per device.

v0:
```python
import jax
import jax.numpy as jnp
from jax import lax
from jax.sharding import PartitionSpec as P


def from_behind(x, axis, by):
    peers = lax.axis_size(axis)
    return lax.ppermute(x, axis, [(i, (i + by) % peers) for i in range(peers)])


def attend(qkv, ctx_grad, slopes, head_dim):
    f32 = jnp.float32
    bf = jnp.bfloat16
    length = qkv.shape[0]
    local = slopes.shape[0]
    qkv = qkv.reshape(length, 3, local, head_dim)
    query, keys, values = (qkv[:, 0], qkv[:, 1], qkv[:, 2])
    scale = head_dim ** (-0.5)
    pos = jnp.arange(length)
    dist = (pos[:, None] - pos[None, :]).astype(f32)
    causal = dist >= 0
    scores = (
        jnp.einsum("qhe,khe->hqk", query, keys, preferred_element_type=f32) * scale
        - slopes[:, None, None] * dist[None]
    )
    scores = jnp.where(causal[None], scores, -1e30)
    top = jnp.max(scores, axis=-1, keepdims=True)
    expo = jnp.where(causal[None], jnp.exp(scores - top), 0.0)
    probs = expo / jnp.sum(expo, axis=-1, keepdims=True)
    probs_b = probs.astype(bf)
    grads = ctx_grad.reshape(length, local, head_dim)
    dprobs = jnp.einsum("qhe,khe->hqk", grads, values, preferred_element_type=f32)
    delta = jnp.sum(probs * dprobs, axis=-1, keepdims=True)
    dscore = (probs * (dprobs - delta) * scale).astype(bf)
    dq = jnp.einsum("hqk,khe->qhe", dscore, keys, preferred_element_type=f32).astype(bf)
    dk = jnp.einsum("hqk,qhe->khe", dscore, query, preferred_element_type=f32).astype(bf)
    dv = jnp.einsum("hqk,qhe->khe", probs_b, grads, preferred_element_type=f32).astype(bf)
    return jnp.stack([dq, dk, dv], axis=1).reshape(length, 3 * local * head_dim)


def on_device(checkpoint, projection, ctx_grad, slopes):
    f32 = jnp.float32
    bf = jnp.bfloat16
    whole = lax.all_gather(checkpoint, "tensor", axis=3, tiled=True)[0, 0]
    features = whole.shape[1]
    columns = 3 * projection.shape[3]
    head_dim = projection.shape[3] // slopes.shape[0]
    grads_in = ctx_grad[0, 0]
    gathered = lax.all_gather(projection, "dp", axis=1, tiled=True)[0].reshape(features, columns)
    qkv = jnp.dot(whole, gathered, preferred_element_type=f32).astype(bf)
    dqkv = attend(qkv, grads_in, slopes, head_dim)
    terms = lax.dot_general(dqkv, gathered, (((1,), (1,)), ((), ())), preferred_element_type=f32)[
        None
    ]
    share = features // lax.axis_size("tensor")
    summed = lax.psum(terms.astype(jnp.bfloat16), "tensor").astype(jnp.float32)
    kept = lax.dynamic_slice_in_dim(summed, lax.axis_index("tensor") * share, share, 2)
    kept = kept.astype(bf)
    return from_behind(kept[None], "pipe", -1)


def solution(mesh):
    placed = (
        P("pipe", "dp", None, "tensor"),
        P("pipe", "dp", None, "tensor"),
        P("pipe", "dp", None, "tensor"),
        P("tensor"),
    )
    return jax.shard_map(
        on_device,
        mesh=mesh,
        in_specs=placed,
        out_specs=P("pipe", "dp", None, "tensor"),
        check_vma=False,
    )
```

profile of v0, /device:TPU:4, one launch (start us, length us, event | category | flops | bytes accessed | tf_op | source)
XLA Modules:
  0.0 623.5 jit_solution(7250117882148818041)
XLA Ops:
  6.5 0.7 all-gather.3.cloned.1.call-update
  7.3 13.5 %copy.11 = bf16[1,1792,3,896]{1,3,2,0:T(8,128)(2,1)} copy(bf16[1,1792,3,896]{3,1,2,0:T(8,128)(2,1)} %param.5) | data formatting | bytes 19267584 | tf_op args[1]
  20.9 0.9 copy-done.1
  21.8 0.4 reshape_squeeze.7
  22.2 0.7 broadcast_compare_fusion
  22.9 53.0 %all-gather.3.cloned.1.call-done = bf16[1,1,192,7168]{3,2,1,0:T(8,128)(2,1)} async-done(((bf16[1,1,192,896]{3,2,1,0:T(8,128)(2,1)}), bf16[1,1,192,7168]{3,2,1,0:T(8,128)(2,1)}) %all-gather.3.cloned.1.call-update) | async-done | bytes 2752528 | tf_op jit(solution)/shard_map/all_gather | solution.py:45
  75.9 338.2 %all-gather.5.cloned.1.call-done = bf16[1,7168,3,896]{1,3,2,0:T(8,128)(2,1)} async-done(((bf16[1,1792,3,896]{1,3,2,0:T(8,128)(2,1)}), bf16[1,7168,3,896]{1,3,2,0:T(8,128)(2,1)}) %all-gather.5.cloned.1.call-update) | async-done | bytes 38535184 | tf_op jit(solution)/shard_map/all_gather | solution.py:50
  414.1 18.8 %convolution_convert_fusion.1 = bf16[192,2688]{1,0:T(8,128)(2,1)S(1)} fusion(bf16[7168,2688]{0,1:T(8,128)(2,1)} %bitcast.50, bf16[1,1,192,7168]{3,2,1,0:T(8,128)(2,1)} %all-gather.3.cloned.1.call-done), kind=kOutput, calls=%fused_computation.4 | convolution fusion | flops 7399268352 | bytes 42319872 | tf_op jit(solution)/shard_map/dot_general | solution.py:51
  432.9 1.3 reshape.34
  434.2 1.0 fusion.46
  435.2 0.4 convolution_bitcast_fusion
  435.5 0.6 copy-done
  436.2 1.9 fusion.47
  438.1 2.4 fusion.30
  440.5 2.4 fusion.27
  442.9 1.7 fusion.26
  444.7 0.7 copy.18
  445.4 1.2 reshape.35
  446.5 17.6 %fusion.2 = bf16[1,192,7168]{2,1,0:T(8,128)(2,1)} fusion(bf16[192,2688]{1,0:T(8,128)(2,1)S(1)} %reshape.35, bf16[7168,2688]{0,1:T(8,128)(2,1)} %bitcast.51), kind=kOutput, calls=%fused_computation.3 | convolution fusion | flops 7400128512 | bytes 42319872 | tf_op jit(solution)/shard_map/dot_general | solution.py:53
  464.2 140.5 %all-reduce.2.cloned.1.call-done = bf16[1,192,7168]{2,1,0:T(8,128)(2,1)} async-done(((bf16[1,192,7168]{2,1,0:T(8,128)(2,1)}), bf16[1,192,7168]{2,1,0:T(8,128)(2,1)}) %all-reduce.2.cloned.1.call-update) | async-done | bytes 2752528 | tf_op jit(solution)/shard_map/psum | solution.py:57
  604.8 1.0 fusion.36
  605.8 3.4 collective-permute-start
  609.2 7.1 %collective-permute-done = bf16[1,1,192,896]{3,2,1,0:T(8,128)(2,1)S(1)} collective-permute-done((bf16[1,1,192,896]{3,2,1,0:T(8,128)(2,1)S(1)}, bf16[1,1,192,896]{3,2,1,0:T(8,128)(2,1)S(1)}, u32[]{:S(2)}, u32[]{:S(2)}) %collective-permute-start) | collective-permute-done | bytes 344096 | tf_op jit(solution)/shard_map/ppermute | solution.py:9
  616.2 0.7 copy.49
  (13 shorter events, 0.3 us)
Async XLA Ops:
  6.5 69.3 %all-gather.3.cloned.1.call-start = ((), (), s32[]{:S(2)}) async-start(), calls=%async_computation | async-start | bytes 3096576 | tf_op jit(solution)/shard_map/all_gather | solution.py:45
  7.3 406.8 %all-gather.5.cloned.1.call-start = ((), (), s32[]{:S(2)}) async-start(), calls=%async_computation.1 | async-start | bytes 48168960 | tf_op jit(solution)/shard_map/all_gather | solution.py:50
  20.8 1.0 copy-start.1
  20.8 583.9 %all-reduce.2.cloned.1.call-start = ((), (), s32[]{:S(2)}) async-start(), calls=%async_computation.2 | async-start | bytes 5505024 | tf_op jit(solution)/shard_map/psum | solution.py:57
  435.2 1.0 copy-start
  435.2 1.0 copy-start.2
  435.2 1.0 copy-start.3
  605.8 10.5 %collective-permute-start = (bf16[1,1,192,896]{3,2,1,0:T(8,128)(2,1)S(1)}, bf16[1,1,192,896]{3,2,1,0:T(8,128)(2,1)S(1)}, u32[]{:S(2)}, u32[]{:S(2)}) collective-permute-start(bf16[1,1,192,896]{3,2,1,0:T(8,128)(2,1)S(1)} %fusion.36), channel_id=1, source_target_pairs={{0,56},{8,0},{16,8},{24,16},{32,24},{40,32},{48,40},{56,48},{1,57}... | collective-permute-start | bytes 1032200 | tf_op jit(solution)/shard_map/ppermute | solution.py:9
Sparse Core Ops, SparseCore 0:
  10.0 65.8 all-gather.2
  77.7 336.3 all-gather.4
  464.3 140.3 all-reduce.1
where the time goes:
time: 624 us; the launch traced here: 623 us
  waiting for transfers between devices  540 us (87%)
  matrix products  45.2 us (7%)
  local copies, waits for them, and re-layouts  20.3 us (3%)
  between operations  13.2 us (2%)
    all_gather x1, waiting for transfers between devices, on_device(): lax.all_gather(projection, 'dp', axis=1, tiled=True)[0]  338 us
    psum x1, waiting for transfers between devices, on_device(): summed = lax.psum(terms.astype(jnp.bfloat16), 'tensor').astype(jnp.float32)  141 us
    all_gather x1, waiting for transfers between devices, on_device(): whole = lax.all_gather(checkpoint, 'tensor', axis=3, tiled=True)[0, 0]  53 us
    dot_general x1, matrix products, on_device(): qkv = jnp.dot(whole, gathered, preferred_element_type=f32).astype(bf)  18.8 us
    dot_general x1, matrix products, on_device(): lax.dot_general(dqkv, gathered, (((1,), (1,)), ((), ())), preferred_eleme...  17.6 us
    unnamed x10, local copies, waits for them, and re-layouts  15.8 us
  transfers between devices with their start and end apart: 4, of which 4 were waited for; matrix products, arithmetic and copies ran while one was open for 2% of the time, Pallas kernels for 0%

commit v1 on v0

v1 whole, which is shorter than its diff:
```python
import functools

import jax
import jax.numpy as jnp
from jax import lax
from jax.experimental import pallas as pl
from jax.experimental.pallas import tpu as pltpu
from jax.sharding import PartitionSpec as P

F32 = jnp.float32
BF = jnp.bfloat16
VMEM = pl.BlockSpec(memory_space=pltpu.VMEM)
SMEM = pl.BlockSpec(memory_space=pltpu.SMEM)
NT = (((1,), (1,)), ((), ()))
TN = (((0,), (0,)), ((), ()))
LIMIT = 48 * 1024 * 1024


def is_root(dp, tensor):
    return (tensor >> 2) == (dp >> 1)


def exchange(value, dp_flip, tensor_flip, senders=None):
    pairs = []
    for dp in range(4):
        for tensor in range(8):
            if senders is None or is_root(dp, tensor) == senders:
                pairs.append((dp * 8 + tensor, (dp ^ dp_flip) * 8 + (tensor ^ tensor_flip)))
    return lax.ppermute(value, ("dp", "tensor"), pairs)


def project_body(where_ref, a_ref, b_ref, c_ref, d_ref, mine_ref, theirs_ref, out_ref, rows_ref):
    width = a_ref.shape[1]
    for slot, ref in enumerate((a_ref, b_ref, c_ref, d_ref)):
        side = where_ref[slot // 2]
        half = where_ref[2 + slot % 2]
        rows_ref[side, :, pl.ds(pl.multiple_of(half * width, 128), width)] = ref[...]
    for part in range(3):
        total = jnp.dot(rows_ref[0], mine_ref[part], preferred_element_type=F32)
        total += jnp.dot(rows_ref[1], theirs_ref[part], preferred_element_type=F32)
        out_ref[part] = total.astype(out_ref.dtype)


def project(where, blocks, mine, theirs, dtype):
    length, width = blocks[0].shape
    return pl.pallas_call(
        project_body,
        out_shape=jax.ShapeDtypeStruct((3, length, width), dtype),
        in_specs=[SMEM] + [VMEM] * 6,
        out_specs=VMEM,
        scratch_shapes=[pltpu.VMEM((2, length, 2 * width), BF)],
        compiler_params=pltpu.CompilerParams(vmem_limit_bytes=LIMIT),
        cost_estimate=pl.CostEstimate(
            flops=2 * length * 4 * width * 3 * width, bytes_accessed=24 * width * width, transcendentals=0
        ),
        name="project",
    )(where, *blocks, mine, theirs)


def attend_body(scale, slopes_ref, mine_ref, theirs_ref, ctx_ref, out_ref):
    length = mine_ref.shape[1]
    head = pl.program_id(0)
    query, keys, values = (
        (mine_ref[part] + theirs_ref[part].astype(F32)).astype(BF) for part in range(3)
    )
    grads = ctx_ref[...]
    rows = lax.broadcasted_iota(jnp.int32, (length, length), 0)
    cols = lax.broadcasted_iota(jnp.int32, (length, length), 1)
    dist = (rows - cols).astype(F32)
    causal = rows >= cols
    scores = lax.dot_general(query, keys, NT, preferred_element_type=F32) * scale - slopes_ref[head] * dist
    scores = jnp.where(causal, scores, -1e30)
    top = jnp.max(scores, axis=-1, keepdims=True)
    expo = jnp.where(causal, jnp.exp(scores - top), 0.0)
    probs = expo / jnp.sum(expo, axis=-1, keepdims=True)
    dprobs = lax.dot_general(grads, values, NT, preferred_element_type=F32)
    delta = jnp.sum(probs * dprobs, axis=-1, keepdims=True)
    dscore = (probs * (dprobs - delta) * scale).astype(BF)
    out_ref[0] = jnp.dot(dscore, keys, preferred_element_type=F32).astype(BF)
    out_ref[1] = lax.dot_general(dscore, query, TN, preferred_element_type=F32).astype(BF)
    out_ref[2] = lax.dot_general(probs.astype(BF), grads, TN, preferred_element_type=F32).astype(BF)


def attend(slopes, mine, theirs, ctx_grad):
    parts, length, width = mine.shape
    heads = slopes.shape[0]
    size = width // heads
    three = pl.BlockSpec((3, length, size), lambda head: (0, 0, head))
    return pl.pallas_call(
        functools.partial(attend_body, size ** (-0.5)),
        out_shape=jax.ShapeDtypeStruct((parts, length, width), BF),
        grid=(heads,),
        in_specs=[SMEM, three, three, pl.BlockSpec((length, size), lambda head: (0, head))],
        out_specs=three,
        compiler_params=pltpu.CompilerParams(vmem_limit_bytes=LIMIT),
        cost_estimate=pl.CostEstimate(
            flops=10 * length * length * width,
            bytes_accessed=14 * length * width,
            transcendentals=heads * length * length,
        ),
        name="attend",
    )(slopes, mine, theirs, ctx_grad)


def back_body(where_ref, dqkv_ref, mine_ref, theirs_ref, keep_ref, send_ref, rows_ref):
    width = dqkv_ref.shape[2]
    for side, ref in enumerate((mine_ref, theirs_ref)):
        for half in range(2):
            total = None
            for part in range(3):
                term = lax.dot_general(
                    dqkv_ref[part],
                    ref[part, half * width : (half + 1) * width, :],
                    NT,
                    preferred_element_type=F32,
                )
                total = term if total is None else total + term
            rows_ref[side, half] = total
    for half in range(2):
        keep_ref[half] = rows_ref[where_ref[0], where_ref[2 + half]]
        send_ref[half] = rows_ref[where_ref[1], where_ref[2 + half]].astype(BF)


def back(where, dqkv, mine, theirs):
    parts, length, width = dqkv.shape
    return pl.pallas_call(
        back_body,
        out_shape=(
            jax.ShapeDtypeStruct((2, length, width), F32),
            jax.ShapeDtypeStruct((2, length, width), BF),
        ),
        in_specs=[SMEM] + [VMEM] * 3,
        out_specs=(VMEM, VMEM),
        scratch_shapes=[pltpu.VMEM((2, 2, length, width), F32)],
        compiler_params=pltpu.CompilerParams(vmem_limit_bytes=LIMIT),
        cost_estimate=pl.CostEstimate(
            flops=2 * length * 4 * width * 3 * width, bytes_accessed=24 * width * width, transcendentals=0
        ),
        name="back",
    )(where, dqkv, mine, theirs)


def on_device(checkpoint, projection, ctx_grad, slopes):
    dp = lax.axis_index("dp")
    tensor = lax.axis_index("tensor")
    core = dp & 1
    column_low = (tensor >> 1) & 1
    own_half = tensor & 1
    root = is_root(dp, tensor)
    side = jnp.where(root, column_low, 1 - column_low) ^ core
    where = jnp.stack([side, 1 - side, own_half, 1 - own_half]).astype(jnp.int32)

    mine = jnp.transpose(projection[0], (1, 0, 2))
    own = checkpoint[0, 0]
    near = exchange(own, 2, 0, False)
    far = exchange(own, 2, 1, False)
    same = exchange(own, 0, 1, True)
    theirs = exchange(mine, 1, 0)

    def spread(value):
        first = jnp.where(root, value, exchange(value, 0, 6, True))
        return first, exchange(first, 0, 2)

    near1, near2 = spread(near)
    far1, far2 = spread(far)
    own1, own2 = spread(own)
    same1, same2 = spread(same)
    sent = project(where, (near1, far1, near2, far2), mine, theirs, BF)
    other = exchange(sent, 2, 0)
    kept = project(where, (own1, same1, own2, same2), mine, theirs, F32)
    dqkv = attend(slopes, kept, other, ctx_grad[0, 0])
    dqkv_other = exchange(dqkv, 2, 0)

    def gather_back(dqkv):
        keep, send = back(where, dqkv, mine, theirs)
        total = keep + exchange(send, 0, 2).astype(F32)
        return total + exchange(total.astype(BF), 0, 6, False).astype(F32)

    grads = gather_back(dqkv)
    result_root = grads[0] + exchange(grads[1].astype(BF), 0, 1, True).astype(F32)
    grads = gather_back(dqkv_other).astype(BF)
    result_rest = exchange(grads[0], 2, 0, True).astype(F32) + exchange(grads[1], 2, 1, True).astype(F32)
    result = jnp.where(root, result_root, result_rest).astype(BF)
    pipe = lax.axis_size("pipe")
    result = lax.ppermute(result, "pipe", [(i, (i - 1) % pipe) for i in range(pipe)])
    return result[None, None]


def solution(mesh):
    placed = (
        P("pipe", "dp", None, "tensor"),
        P("pipe", "dp", None, "tensor"),
        P("pipe", "dp", None, "tensor"),
        P("tensor"),
    )
    return jax.shard_map(
        on_device,
        mesh=mesh,
        in_specs=placed,
        out_specs=P("pipe", "dp", None, "tensor"),
        check_vma=False,
    )
```

time: 624 us -> 174 us (0.28)
  waiting for transfers between devices: 540 us -> 75.3 us
  Pallas kernels: 0 us -> 54.5 us
  matrix products: 45.2 us -> 0 us
  starting transfers between devices: 3.47 us -> 40.9 us
  local copies, waits for them, and re-layouts: 20.3 us -> 0.84 us
  between operations: 13.2 us -> 0.3 us
    all_gather x2 -> x0, waiting for transfers between devices: 391 us -> none  [the longest x1 338 us: on_device(): lax.all_gather(projection, 'dp', axis=1, tiled=True)[0]]
    psum x1 -> x0, waiting for transfers between devices: 141 us -> none  [on_device(): summed = lax.psum(terms.astype(jnp.bfloat16), 'tensor').astype(jnp.float32)]
    ppermute x1 -> x22, waiting for transfers between devices: 7.08 us -> 75.3 us  [the longest x21 70.5 us: exchange(): return lax.ppermute(value, ('dp', 'tensor'), pairs)]
    pallas_call x0 -> x5, Pallas kernels: none -> 54.5 us  [the longest x2 26.2 us: back(): pl.pallas_call(back_body, out_shape=(jax.ShapeDtypeStruct((2, length, wid...]
    dot_general x6 -> x0, matrix products: 43.3 us -> none  [the longest x1 18.8 us: on_device(): qkv = jnp.dot(whole, gathered, preferred_element_type=f32).astype(bf)]
    ppermute x1 -> x22, starting transfers between devices: 3.39 us -> 40.9 us  [the longest x21 35 us: exchange(): return lax.ppermute(value, ('dp', 'tensor'), pairs)]
    unnamed x10 -> x7, local copies, waits for them, and re-layouts: 15.8 us -> 0.75 us
  transfers between devices with their start and end apart: 4 -> 22, of which waited for: 4 -> 14; matrix products, arithmetic and copies ran while one was open for 2% -> 1% of each run, Pallas kernels for 0% -> 28%
where the time goes in v1:
time: 174 us; the launch traced here: 173 us
  waiting for transfers between devices  75.3 us (43%)
  Pallas kernels  54.5 us (31%)
  starting transfers between devices  40.9 us (24%)
    ppermute x21, waiting for transfers between devices, exchange(): return lax.ppermute(value, ('dp', 'tensor'), pairs)  70.5 us
    ppermute x21, starting transfers between devices, exchange(): return lax.ppermute(value, ('dp', 'tensor'), pairs)  35 us
    pallas_call x2, Pallas kernels, back(): pl.pallas_call(back_body, out_shape=(jax.ShapeDtypeStruct((2, length, wid...  26.2 us
    pallas_call x2, Pallas kernels, project(): pl.pallas_call(project_body, out_shape=jax.ShapeDtypeStruct((3, length, w...  22.1 us
    pallas_call x1, Pallas kernels, attend(): pl.pallas_call(functools.partial(attend_body, size ** (-0.5)), out_shape=...  6.21 us
    ppermute x1, starting transfers between devices, on_device(): lax.ppermute(result, 'pipe', [(i, (i - 1) % pipe) for i in range(pipe)])  5.92 us
    ppermute x1, waiting for transfers between devices, on_device(): lax.ppermute(result, 'pipe', [(i, (i - 1) % pipe) for i in range(pipe)])  4.77 us
  transfers between devices with their start and end apart: 22, of which 14 were waited for; matrix products, arithmetic and copies ran while one was open for 1% of the time, Pallas kernels for 28%

profile of v1, /device:TPU:4, one launch (start us, length us, event | category | flops | bytes accessed | tf_op | source)
XLA Modules:
  0.0 173.0 jit_solution(12582746872888448129)
XLA Ops:
  0.0 3.6 %collective-permute-start.6 = (bf16[192,896]{1,0:T(8,128)(2,1)}, bf16[192,896]{1,0:T(8,128)(2,1)S(1)}, u32[]{:S(2)}, u32[]{:S(2)}) collective-permute-start(bf16[192,896]{1,0:T(8,128)(2,1)} %bitcast.31), channel_id=1, source_target_pairs={{4,132},{5,133},{6,134},{7,135},{68,196},{69,197},{70,198},{71,199... | collective-permute-start | bytes 1032200 | tf_op jit(solution)/shard_map/ppermute | solution.py:29
  3.7 2.7 %collective-permute-start.8 = (bf16[192,896]{1,0:T(8,128)(2,1)}, bf16[192,896]{1,0:T(8,128)(2,1)S(1)}, u32[]{:S(2)}, u32[]{:S(2)}) collective-permute-start(bf16[192,896]{1,0:T(8,128)(2,1)} %bitcast.32), channel_id=1, source_target_pairs={{4,133},{5,132},{6,135},{7,134},{68,197},{69,196},{70,199},{71,198... | collective-permute-start | bytes 1032200 | tf_op jit(solution)/shard_map/ppermute | solution.py:29
  6.4 5.4 %collective-permute-done.6 = bf16[192,896]{1,0:T(8,128)(2,1)S(1)} collective-permute-done((bf16[192,896]{1,0:T(8,128)(2,1)}, bf16[192,896]{1,0:T(8,128)(2,1)S(1)}, u32[]{:S(2)}, u32[]{:S(2)}) %collective-permute-start.6) | collective-permute-done | bytes 344096 | tf_op jit(solution)/shard_map/ppermute | solution.py:29
  16.5 8.1 %collective-permute-done.7 = bf16[192,896]{1,0:T(8,128)(2,1)S(1)} collective-permute-done((bf16[192,896]{1,0:T(8,128)(2,1)S(1)}, bf16[192,896]{1,0:T(8,128)(2,1)S(1)}, u32[]{:S(2)}, u32[]{:S(2)}) %collective-permute-start.7) | collective-permute-done | bytes 344096 | tf_op jit(solution)/shard_map/ppermute | solution.py:29
  24.7 2.5 %collective-permute-start.10 = (bf16[192,896]{1,0:T(8,128)(2,1)S(1)}, bf16[192,896]{1,0:T(8,128)(2,1)S(1)}, u32[]{:S(2)}, u32[]{:S(2)}) collective-permute-start(bf16[192,896]{1,0:T(8,128)(2,1)S(1)} %broadcast_select_fusion.1.a_ref), channel_id=1, source_target_pairs={{0,2},{1,3},{2,0},{3,1},{4,6},{5,7},{6,4},{7,5},{64,66},{65,67},{6... | collective-permute-start | bytes 1032200 | tf_op jit(solution)/shard_map/ppermute | solution.py:29
  27.2 3.4 %collective-permute-done.9 = bf16[192,896]{1,0:T(8,128)(2,1)S(1)} collective-permute-done((bf16[192,896]{1,0:T(8,128)(2,1)S(1)}, bf16[192,896]{1,0:T(8,128)(2,1)S(1)}, u32[]{:S(2)}, u32[]{:S(2)}) %collective-permute-start.9) | collective-permute-done | bytes 344096 | tf_op jit(solution)/shard_map/ppermute | solution.py:29
  30.6 2.5 %collective-permute-start.11 = (bf16[192,896]{1,0:T(8,128)(2,1)S(1)}, bf16[192,896]{1,0:T(8,128)(2,1)S(1)}, u32[]{:S(2)}, u32[]{:S(2)}) collective-permute-start(bf16[192,896]{1,0:T(8,128)(2,1)S(1)} %broadcast_select_fusion.b_ref), channel_id=1, source_target_pairs={{0,2},{1,3},{2,0},{3,1},{4,6},{5,7},{6,4},{7,5},{64,66},{65,67},{6... | collective-permute-start | bytes 1032200 | tf_op jit(solution)/shard_map/ppermute | solution.py:29
  35.8 4.2 %collective-permute-done.11.d_ref = bf16[192,896]{1,0:T(8,128)(2,1)S(1)} collective-permute-done((bf16[192,896]{1,0:T(8,128)(2,1)S(1)}, bf16[192,896]{1,0:T(8,128)(2,1)S(1)}, u32[]{:S(2)}, u32[]{:S(2)}) %collective-permute-start.11) | collective-permute-done | bytes 344096 | tf_op jit(solution)/shard_map/ppermute | solution.py:29
  40.0 11.0 %project.3 = bf16[3,192,896]{2,1,0:T(8,128)(2,1)S(1)} custom-call(s32[4]{0:T(128)S(1)} %pad_add_fusion.where_ref, bf16[192,896]{1,0:T(8,128)(2,1)S(1)} %broadcast_select_fusion.1.a_ref, bf16[192,896]{1,0:T(8,128)(2,1)S(1)} %broadcast_select_fusion.b_ref, bf16[192,896]{1,0:T(8,128)(2,1)S(1)} %collective-permute-done.10.c_ref, ...), custom_call_target="tpu_custom_call" | custom-call | flops 3699376128 | bytes 19267584 | tf_op jit(solution)/shard_map/project/pallas_call | solution.py:46
  53.6 8.6 %collective-permute-done.3.c_ref = bf16[192,896]{1,0:T(8,128)(2,1)S(1)} collective-permute-done((bf16[192,896]{1,0:T(8,128)(2,1)S(1)}, bf16[192,896]{1,0:T(8,128)(2,1)S(1)}, u32[]{:S(2)}, u32[]{:S(2)}) %collective-permute-start.3) | collective-permute-done | bytes 344096 | tf_op jit(solution)/shard_map/ppermute | solution.py:29
  62.2 4.3 %collective-permute-done.4.d_ref = bf16[192,896]{1,0:T(8,128)(2,1)S(1)} collective-permute-done((bf16[192,896]{1,0:T(8,128)(2,1)S(1)}, bf16[192,896]{1,0:T(8,128)(2,1)S(1)}, u32[]{:S(2)}, u32[]{:S(2)}) %collective-permute-start.4) | collective-permute-done | bytes 344096 | tf_op jit(solution)/shard_map/ppermute | solution.py:29
  66.6 11.0 %project.2.mine_ref = f32[3,192,896]{2,1,0:T(8,128)S(1)} custom-call(s32[4]{0:T(128)S(1)} %pad_add_fusion.where_ref, bf16[192,896]{1,0:T(8,128)(2,1)S(1)} %broadcast_select_fusion.3.a_ref, bf16[192,896]{1,0:T(8,128)(2,1)S(1)} %broadcast_select_fusion.2.b_ref, bf16[192,896]{1,0:T(8,128)(2,1)S(1)} %collective-permute-done.3.c_ref, ...), custom_call_target="tpu_custom_call" | custom-call | flops 3699376128 | bytes 19267584 | tf_op jit(solution)/shard_map/project/pallas_call | solution.py:46
  77.6 6.2 %attend.1.dqkv_ref = bf16[3,192,896]{2,1,0:T(8,128)(2,1)S(1)} custom-call(f32[7]{0:T(128)S(1)} %copy-done.1, f32[3,192,896]{2,1,0:T(8,128)S(1)} %project.2.mine_ref, bf16[3,192,896]{2,1,0:T(8,128)(2,1)S(1)} %collective-permute-done.12.theirs_ref, bf16[192,896]{1,0:T(8,128)(2,1)S(1)} %bitcast.25), custom_call_target="tpu_custom_call" | custom-call | flops 330301440 | bytes 2408448 | tf_op jit(solution)/shard_map/attend/pallas_call | solution.py:89
  85.7 13.1 %back.2 = (f32[2,192,896]{2,1,0:T(8,128)S(1)}, bf16[2,192,896]{2,1,0:T(8,128)(2,1)S(1)}) custom-call(s32[4]{0:T(128)S(1)} %pad_add_fusion.where_ref, bf16[3,192,896]{2,1,0:T(8,128)(2,1)S(1)} %attend.1.dqkv_ref, bf16[3,1792,896]{2,1,0:T(8,128)(2,1)} %bitcast.29, bf16[3,1792,896]{2,1,0:T(8,128)(2,1)} %collective-permute-done.5.theirs_ref), custom_call_target="tpu_custom_call" | custom-call | flops 3699376128 | bytes 19267584 | tf_op jit(solution)/shard_map/back/pallas_call | solution.py:126
  100.8 4.9 %collective-permute-done.16.dqkv_ref = bf16[3,192,896]{2,1,0:T(8,128)(2,1)S(1)} collective-permute-done((bf16[3,192,896]{2,1,0:T(8,128)(2,1)S(1)}, bf16[3,192,896]{2,1,0:T(8,128)(2,1)S(1)}, u32[]{:S(2)}, u32[]{:S(2)}) %collective-permute-start.16) | collective-permute-done | bytes 1032224 | tf_op jit(solution)/shard_map/ppermute | solution.py:29
  105.7 13.1 %back.3 = (f32[2,192,896]{2,1,0:T(8,128)S(1)}, bf16[2,192,896]{2,1,0:T(8,128)(2,1)S(1)}) custom-call(s32[4]{0:T(128)S(1)} %pad_add_fusion.where_ref, bf16[3,192,896]{2,1,0:T(8,128)(2,1)S(1)} %collective-permute-done.16.dqkv_ref, bf16[3,1792,896]{2,1,0:T(8,128)(2,1)} %bitcast.30, bf16[3,1792,896]{2,1,0:T(8,128)(2,1)} %collective-permute-done.5.theirs_ref), custom_call_target="tpu_custom_call" | custom-call | flops 3699376128 | bytes 19267584 | tf_op jit(solution)/shard_map/back/pallas_call | solution.py:126
  120.6 3.4 %collective-permute-start.14 = (bf16[2,192,896]{2,1,0:T(8,128)(2,1)S(1)}, bf16[2,192,896]{2,1,0:T(8,128)(2,1)S(1)}, u32[]{:S(2)}, u32[]{:S(2)}) collective-permute-start(bf16[2,192,896]{2,1,0:T(8,128)(2,1)S(1)} %fusion), channel_id=1, source_target_pairs={{4,2},{5,3},{6,0},{7,1},{68,66},{69,67},{70,64},{71,65},{128,134},... | collective-permute-start | bytes 2064392 | tf_op jit(solution)/shard_map/ppermute | solution.py:29
  124.0 8.4 %collective-permute-done.17 = bf16[2,192,896]{2,1,0:T(8,128)(2,1)S(1)} collective-permute-done((bf16[2,192,896]{2,1,0:T(8,128)(2,1)S(1)}, bf16[2,192,896]{2,1,0:T(8,128)(2,1)S(1)}, u32[]{:S(2)}, u32[]{:S(2)}) %collective-permute-start.17) | collective-permute-done | bytes 688160 | tf_op jit(solution)/shard_map/ppermute | solution.py:29
  132.6 3.2 %collective-permute-start.18 = (bf16[2,192,896]{2,1,0:T(8,128)(2,1)S(1)}, bf16[2,192,896]{2,1,0:T(8,128)(2,1)S(1)}, u32[]{:S(2)}, u32[]{:S(2)}) collective-permute-start(bf16[2,192,896]{2,1,0:T(8,128)(2,1)S(1)} %fusion.1), channel_id=1, source_target_pairs={{4,2},{5,3},{6,0},{7,1},{68,66},{69,67},{70,64},{71,65},{128,134},... | collective-permute-start | bytes 2064392 | tf_op jit(solution)/shard_map/ppermute | solution.py:29
  138.6 10.4 %collective-permute-done.18 = bf16[2,192,896]{2,1,0:T(8,128)(2,1)S(1)} collective-permute-done((bf16[2,192,896]{2,1,0:T(8,128)(2,1)S(1)}, bf16[2,192,896]{2,1,0:T(8,128)(2,1)S(1)}, u32[]{:S(2)}, u32[]{:S(2)}) %collective-permute-start.18) | collective-permute-done | bytes 688160 | tf_op jit(solution)/shard_map/ppermute | solution.py:29
  151.9 6.5 %collective-permute-done.19 = bf16[192,896]{1,0:T(8,128)(2,1)S(1)} collective-permute-done((bf16[192,896]{1,0:T(8,128)(2,1)S(1)}, bf16[192,896]{1,0:T(8,128)(2,1)S(1)}, u32[]{:S(2)}, u32[]{:S(2)}) %collective-permute-start.19) | collective-permute-done | bytes 344096 | tf_op jit(solution)/shard_map/ppermute | solution.py:29
  158.4 3.0 %collective-permute-done.20 = bf16[192,896]{1,0:T(8,128)(2,1)S(1)} collective-permute-done((bf16[192,896]{1,0:T(8,128)(2,1)S(1)}, bf16[192,896]{1,0:T(8,128)(2,1)S(1)}, u32[]{:S(2)}, u32[]{:S(2)}) %collective-permute-start.20) | collective-permute-done | bytes 344096 | tf_op jit(solution)/shard_map/ppermute | solution.py:29
  161.6 5.9 %collective-permute-start.21 = (bf16[192,896]{1,0:T(8,128)(2,1)S(1)}, bf16[192,896]{1,0:T(8,128)(2,1)S(1)}, u32[]{:S(2)}, u32[]{:S(2)}) collective-permute-start(bf16[192,896]{1,0:T(8,128)(2,1)S(1)} %fusion.4), channel_id=1, source_target_pairs={{0,56},{8,0},{16,8},{24,16},{32,24},{40,32},{48,40},{56,48},{1,57}... | collective-permute-start | bytes 1032200 | tf_op jit(solution)/shard_map/ppermute | solution.py:185
  167.5 4.8 %collective-permute-done.21 = bf16[192,896]{1,0:T(8,128)(2,1)S(1)} collective-permute-done((bf16[192,896]{1,0:T(8,128)(2,1)S(1)}, bf16[192,896]{1,0:T(8,128)(2,1)S(1)}, u32[]{:S(2)}, u32[]{:S(2)}) %collective-permute-start.21) | collective-permute-done | bytes 344096 | tf_op jit(solution)/shard_map/ppermute | solution.py:185
  (44 shorter events, 22.3 us)
Async XLA Ops:
  0.0 33.1 %copy-start.2 = (bf16[1,1,192,896]{3,2,1,0:T(8,128)(2,1)S(1)}, bf16[1,1,192,896]{3,2,1,0:T(8,128)(2,1)}, u32[]{:S(2)}) copy-start(bf16[1,1,192,896]{3,2,1,0:T(8,128)(2,1)} %param.4) | copy-start | bytes 1032196
  0.0 40.0 %collective-permute-start.5 = (bf16[3,1792,896]{2,1,0:T(8,128)(2,1)}, bf16[3,1792,896]{2,1,0:T(8,128)(2,1)}, u32[]{:S(2)}, u32[]{:S(2)}) collective-permute-start(bf16[3,1792,896]{2,1,0:T(8,128)(2,1)} %bitcast.26), channel_id=1, source_target_pairs={{0,64},{1,65},{2,66},{3,67},{4,68},{5,69},{6,70},{7,71},{64,0},{65... | collective-permute-start | bytes 28901384 | tf_op jit(solution)/shard_map/ppermute | solution.py:29
  0.0 11.8 %collective-permute-start.6 = (bf16[192,896]{1,0:T(8,128)(2,1)}, bf16[192,896]{1,0:T(8,128)(2,1)S(1)}, u32[]{:S(2)}, u32[]{:S(2)}) collective-permute-start(bf16[192,896]{1,0:T(8,128)(2,1)} %bitcast.31), channel_id=1, source_target_pairs={{4,132},{5,133},{6,134},{7,135},{68,196},{69,197},{70,198},{71,199... | collective-permute-start | bytes 1032200 | tf_op jit(solution)/shard_map/ppermute | solution.py:29
  3.7 10.9 %collective-permute-start.8 = (bf16[192,896]{1,0:T(8,128)(2,1)}, bf16[192,896]{1,0:T(8,128)(2,1)S(1)}, u32[]{:S(2)}, u32[]{:S(2)}) collective-permute-start(bf16[192,896]{1,0:T(8,128)(2,1)} %bitcast.32), channel_id=1, source_target_pairs={{4,133},{5,132},{6,135},{7,134},{68,197},{69,196},{70,199},{71,198... | collective-permute-start | bytes 1032200 | tf_op jit(solution)/shard_map/ppermute | solution.py:29
  11.8 12.9 %collective-permute-start.7 = (bf16[192,896]{1,0:T(8,128)(2,1)S(1)}, bf16[192,896]{1,0:T(8,128)(2,1)S(1)}, u32[]{:S(2)}, u32[]{:S(2)}) collective-permute-start(bf16[192,896]{1,0:T(8,128)(2,1)S(1)} %collective-permute-done.6), channel_id=1, source_target_pairs={{0,6},{1,7},{2,4},{3,5},{64,70},{65,71},{66,68},{67,69},{132,130},... | collective-permute-start | bytes 1032200 | tf_op jit(solution)/shard_map/ppermute | solution.py:29
  14.5 16.0 %collective-permute-start.9 = (bf16[192,896]{1,0:T(8,128)(2,1)S(1)}, bf16[192,896]{1,0:T(8,128)(2,1)S(1)}, u32[]{:S(2)}, u32[]{:S(2)}) collective-permute-start(bf16[192,896]{1,0:T(8,128)(2,1)S(1)} %collective-permute-done.8), channel_id=1, source_target_pairs={{0,6},{1,7},{2,4},{3,5},{64,70},{65,71},{66,68},{67,69},{132,130},... | collective-permute-start | bytes 1032200 | tf_op jit(solution)/shard_map/ppermute | solution.py:29
  15.8 18.7 %collective-permute-start.1 = (bf16[192,896]{1,0:T(8,128)(2,1)}, bf16[192,896]{1,0:T(8,128)(2,1)S(1)}, u32[]{:S(2)}, u32[]{:S(2)}) collective-permute-start(bf16[192,896]{1,0:T(8,128)(2,1)} %bitcast.33), channel_id=1, source_target_pairs={{0,1},{1,0},{2,3},{3,2},{64,65},{65,64},{66,67},{67,66},{132,133},... | collective-permute-start | bytes 1032200 | tf_op jit(solution)/shard_map/ppermute | solution.py:29
  24.7 11.1 %collective-permute-start.10 = (bf16[192,896]{1,0:T(8,128)(2,1)S(1)}, bf16[192,896]{1,0:T(8,128)(2,1)S(1)}, u32[]{:S(2)}, u32[]{:S(2)}) collective-permute-start(bf16[192,896]{1,0:T(8,128)(2,1)S(1)} %broadcast_select_fusion.1.a_ref), channel_id=1, source_target_pairs={{0,2},{1,3},{2,0},{3,1},{4,6},{5,7},{6,4},{7,5},{64,66},{65,67},{6... | collective-permute-start | bytes 1032200 | tf_op jit(solution)/shard_map/ppermute | solution.py:29
  30.6 9.4 %collective-permute-start.11 = (bf16[192,896]{1,0:T(8,128)(2,1)S(1)}, bf16[192,896]{1,0:T(8,128)(2,1)S(1)}, u32[]{:S(2)}, u32[]{:S(2)}) collective-permute-start(bf16[192,896]{1,0:T(8,128)(2,1)S(1)} %broadcast_select_fusion.b_ref), channel_id=1, source_target_pairs={{0,2},{1,3},{2,0},{3,1},{4,6},{5,7},{6,4},{7,5},{64,66},{65,67},{6... | collective-permute-start | bytes 1032200 | tf_op jit(solution)/shard_map/ppermute | solution.py:29
  33.1 18.0 %collective-permute-start = (bf16[192,896]{1,0:T(8,128)(2,1)S(1)}, bf16[192,896]{1,0:T(8,128)(2,1)S(1)}, u32[]{:S(2)}, u32[]{:S(2)}) collective-permute-start(bf16[192,896]{1,0:T(8,128)(2,1)S(1)} %bitcast.34), channel_id=1, source_target_pairs={{0,6},{1,7},{2,4},{3,5},{64,70},{65,71},{66,68},{67,69},{132,130},... | collective-permute-start | bytes 1032200 | tf_op jit(solution)/shard_map/ppermute | solution.py:29
  34.5 18.6 %collective-permute-start.2 = (bf16[192,896]{1,0:T(8,128)(2,1)S(1)}, bf16[192,896]{1,0:T(8,128)(2,1)S(1)}, u32[]{:S(2)}, u32[]{:S(2)}) collective-permute-start(bf16[192,896]{1,0:T(8,128)(2,1)S(1)} %collective-permute-done.1), channel_id=1, source_target_pairs={{0,6},{1,7},{2,4},{3,5},{64,70},{65,71},{66,68},{67,69},{132,130},... | collective-permute-start | bytes 1032200 | tf_op jit(solution)/shard_map/ppermute | solution.py:29
  51.0 26.6 %collective-permute-start.12 = (bf16[3,192,896]{2,1,0:T(8,128)(2,1)S(1)}, bf16[3,192,896]{2,1,0:T(8,128)(2,1)S(1)}, u32[]{:S(2)}, u32[]{:S(2)}) collective-permute-start(bf16[3,192,896]{2,1,0:T(8,128)(2,1)S(1)} %project.3), channel_id=1, source_target_pairs={{0,128},{1,129},{2,130},{3,131},{4,132},{5,133},{6,134},{7,135},{6... | collective-permute-start | bytes 3096584 | tf_op jit(solution)/shard_map/ppermute | solution.py:29
  51.2 11.1 %collective-permute-start.3 = (bf16[192,896]{1,0:T(8,128)(2,1)S(1)}, bf16[192,896]{1,0:T(8,128)(2,1)S(1)}, u32[]{:S(2)}, u32[]{:S(2)}) collective-permute-start(bf16[192,896]{1,0:T(8,128)(2,1)S(1)} %broadcast_select_fusion.3.a_ref), channel_id=1, source_target_pairs={{0,2},{1,3},{2,0},{3,1},{4,6},{5,7},{6,4},{7,5},{64,66},{65,67},{6... | collective-permute-start | bytes 1032200 | tf_op jit(solution)/shard_map/ppermute | solution.py:29
  53.1 24.5 %copy-start = (bf16[1,1,192,896]{3,2,1,0:T(8,128)(2,1)S(1)}, bf16[1,1,192,896]{3,2,1,0:T(8,128)(2,1)}, u32[]{:S(2)}) copy-start(bf16[1,1,192,896]{3,2,1,0:T(8,128)(2,1)} %param.6) | copy-start | bytes 1032196
  53.2 13.4 %collective-permute-start.4 = (bf16[192,896]{1,0:T(8,128)(2,1)S(1)}, bf16[192,896]{1,0:T(8,128)(2,1)S(1)}, u32[]{:S(2)}, u32[]{:S(2)}) collective-permute-start(bf16[192,896]{1,0:T(8,128)(2,1)S(1)} %broadcast_select_fusion.2.b_ref), channel_id=1, source_target_pairs={{0,2},{1,3},{2,0},{3,1},{4,6},{5,7},{6,4},{7,5},{64,66},{65,67},{6... | collective-permute-start | bytes 1032200 | tf_op jit(solution)/shard_map/ppermute | solution.py:29
  83.9 21.9 %collective-permute-start.16 = (bf16[3,192,896]{2,1,0:T(8,128)(2,1)S(1)}, bf16[3,192,896]{2,1,0:T(8,128)(2,1)S(1)}, u32[]{:S(2)}, u32[]{:S(2)}) collective-permute-start(bf16[3,192,896]{2,1,0:T(8,128)(2,1)S(1)} %attend.1.dqkv_ref), channel_id=1, source_target_pairs={{0,128},{1,129},{2,130},{3,131},{4,132},{5,133},{6,134},{7,135},{6... | collective-permute-start | bytes 3096584 | tf_op jit(solution)/shard_map/ppermute | solution.py:29
  98.8 21.7 %collective-permute-start.13 = (bf16[2,192,896]{2,1,0:T(8,128)(2,1)S(1)}, bf16[2,192,896]{2,1,0:T(8,128)(2,1)S(1)}, u32[]{:S(2)}, u32[]{:S(2)}) collective-permute-start(bf16[2,192,896]{2,1,0:T(8,128)(2,1)S(1)} %get-tuple-element.10), channel_id=1, source_target_pairs={{0,2},{1,3},{2,0},{3,1},{4,6},{5,7},{6,4},{7,5},{64,66},{65,67},{6... | collective-permute-start | bytes 2064392 | tf_op jit(solution)/shard_map/ppermute | solution.py:29
  118.8 13.6 %collective-permute-start.17 = (bf16[2,192,896]{2,1,0:T(8,128)(2,1)S(1)}, bf16[2,192,896]{2,1,0:T(8,128)(2,1)S(1)}, u32[]{:S(2)}, u32[]{:S(2)}) collective-permute-start(bf16[2,192,896]{2,1,0:T(8,128)(2,1)S(1)} %get-tuple-element.12), channel_id=1, source_target_pairs={{0,2},{1,3},{2,0},{3,1},{4,6},{5,7},{6,4},{7,5},{64,66},{65,67},{6... | collective-permute-start | bytes 2064392 | tf_op jit(solution)/shard_map/ppermute | solution.py:29
  120.6 16.9 %collective-permute-start.14 = (bf16[2,192,896]{2,1,0:T(8,128)(2,1)S(1)}, bf16[2,192,896]{2,1,0:T(8,128)(2,1)S(1)}, u32[]{:S(2)}, u32[]{:S(2)}) collective-permute-start(bf16[2,192,896]{2,1,0:T(8,128)(2,1)S(1)} %fusion), channel_id=1, source_target_pairs={{4,2},{5,3},{6,0},{7,1},{68,66},{69,67},{70,64},{71,65},{128,134},... | collective-permute-start | bytes 2064392 | tf_op jit(solution)/shard_map/ppermute | solution.py:29
  132.6 16.4 %collective-permute-start.18 = (bf16[2,192,896]{2,1,0:T(8,128)(2,1)S(1)}, bf16[2,192,896]{2,1,0:T(8,128)(2,1)S(1)}, u32[]{:S(2)}, u32[]{:S(2)}) collective-permute-start(bf16[2,192,896]{2,1,0:T(8,128)(2,1)S(1)} %fusion.1), channel_id=1, source_target_pairs={{4,2},{5,3},{6,0},{7,1},{68,66},{69,67},{70,64},{71,65},{128,134},... | collective-permute-start | bytes 2064392 | tf_op jit(solution)/shard_map/ppermute | solution.py:29
  137.9 14.0 %collective-permute-start.15 = (bf16[192,896]{1,0:T(8,128)(2,1)S(1)}, bf16[192,896]{1,0:T(8,128)(2,1)S(1)}, u32[]{:S(2)}, u32[]{:S(2)}) collective-permute-start(bf16[192,896]{1,0:T(8,128)(2,1)S(1)} %fusion.5), channel_id=1, source_target_pairs={{0,1},{1,0},{2,3},{3,2},{64,65},{65,64},{66,67},{67,66},{132,133},... | collective-permute-start | bytes 1032200 | tf_op jit(solution)/shard_map/ppermute | solution.py:29
  149.3 9.1 %collective-permute-start.19 = (bf16[192,896]{1,0:T(8,128)(2,1)S(1)}, bf16[192,896]{1,0:T(8,128)(2,1)S(1)}, u32[]{:S(2)}, u32[]{:S(2)}) collective-permute-start(bf16[192,896]{1,0:T(8,128)(2,1)S(1)} %get-tuple-element.13), channel_id=1, source_target_pairs={{0,128},{1,129},{2,130},{3,131},{64,192},{65,193},{66,194},{67,195... | collective-permute-start | bytes 1032200 | tf_op jit(solution)/shard_map/ppermute | solution.py:29
  150.6 10.8 %collective-permute-start.20 = (bf16[192,896]{1,0:T(8,128)(2,1)S(1)}, bf16[192,896]{1,0:T(8,128)(2,1)S(1)}, u32[]{:S(2)}, u32[]{:S(2)}) collective-permute-start(bf16[192,896]{1,0:T(8,128)(2,1)S(1)} %get-tuple-element.14), channel_id=1, source_target_pairs={{0,129},{1,128},{2,131},{3,130},{64,193},{65,192},{66,195},{67,194... | collective-permute-start | bytes 1032200 | tf_op jit(solution)/shard_map/ppermute | solution.py:29
  161.6 10.7 %collective-permute-start.21 = (bf16[192,896]{1,0:T(8,128)(2,1)S(1)}, bf16[192,896]{1,0:T(8,128)(2,1)S(1)}, u32[]{:S(2)}, u32[]{:S(2)}) collective-permute-start(bf16[192,896]{1,0:T(8,128)(2,1)S(1)} %fusion.4), channel_id=1, source_target_pairs={{0,56},{8,0},{16,8},{24,16},{32,24},{40,32},{48,40},{56,48},{1,57}... | collective-permute-start | bytes 1032200 | tf_op jit(solution)/shard_map/ppermute | solution.py:185
  (1 other events, 24.5 us)
